TPU v7x, 512 devices: a whole 4x8x8 slice. The times are simulated.
512 devices in a mesh: leaf: 32 (over x, y), tile: 16 (over z, core).
Axes of the slice: x: 4, y: 8, z: 8, core: 2. Of those that a mesh axis runs over, the one named last changes fastest.
Arguments:
- parent_cov: float32 [4, 2048, 2048], P(None, 'tile', 'leaf'), as said below
- parent_map: int32 [32], P('leaf'), may hold values from 0 to 3
- front_rows: int32 [32, 2], P('leaf'), may hold values from 1024 to 1536, as said below
- rows_mid: int32 [32, 1536], P('leaf'), may hold values from 0 to 2047, as said below
- rows_low: int32 [32, 1536], P('leaf'), may hold values from 0 to 2047, as said below
- factor_mid: float32 [32, 1536, 512], P('leaf', 'tile'), may hold values from -0.15625 to 0.15625
- dinv_mid: float32 [32, 512, 512], P('leaf', 'tile'), as said below
- factor_low: float32 [32, 1536, 512], P('leaf', 'tile'), may hold values from -0.15625 to 0.15625
- diag_low: float32 [32, 512], P('leaf', 'tile'), may hold values from 0.5 to 2
Outputs:
- variance_mid: float32 [32, 512], P('leaf', 'tile')
- variance_low: float32 [32, 512], P('leaf', 'tile')
Inputs may be any that keep to these rules, and one draw needn't show every extreme that they name: Each parent_cov[p] is exactly symmetric. Each dinv_mid[g] is exactly symmetric. `front_rows`: some group has 1536 live rows in both columns. `rows_mid`: each row holds 1536 distinct positions in increasing order. `rows_low`: row g holds 1536 distinct positions in increasing order, all below 512 + front_rows[g, 0].
All inputs are finite; a program needn't handle non-finite values.
Results may differ from a plain program's by a relative error of at most 0.0003.
Values sent between devices are 32-bit elements; how exact they have to be, the bound alone decides.
A program may use at most 64 MiB of HBM per device.

v0:
```python
import jax
import jax.numpy as jnp
from jax import lax
from jax.sharding import PartitionSpec as P

EXACT_PRECISION = lax.Precision.HIGHEST


def matmul(left, right):
    return jnp.dot(left, right, precision=EXACT_PRECISION, preferred_element_type=jnp.float32)


def inner_rows(left, right):
    return lax.dot_general(
        left,
        right,
        (((0,), (0,)), ((), ())),
        precision=EXACT_PRECISION,
        preferred_element_type=jnp.float32,
    )


def apply_factor(matrix, running, shard_piece):
    return running - matmul(matrix, shard_piece)


def body(
    parent_cov,
    parent_map,
    front_rows,
    rows_mid,
    rows_low,
    factor_mid,
    dinv_mid,
    factor_low,
    diag_low,
):
    tile_count = lax.axis_size("tile")
    position = lax.axis_index("tile")
    supernode = dinv_mid.shape[2]
    update = rows_mid.shape[1]
    kk_share = supernode // tile_count
    rr_share = update // tile_count
    mid_list = rows_mid[0]
    low_list = rows_low[0]
    live_mid = (jnp.arange(update) < front_rows[0, 0]).astype(jnp.float32)
    live_low = (jnp.arange(update) < front_rows[0, 1]).astype(jnp.float32)
    chosen = lax.dynamic_index_in_dim(
        lax.all_gather(parent_cov, "leaf", axis=2, tiled=True), parent_map[0], 0, keepdims=False
    )
    width = chosen.shape[1]
    inside = jnp.logical_and(mid_list >= 0, mid_list < width).astype(jnp.float32)
    picked = jnp.take(chosen, jnp.clip(mid_list, 0, width - 1), axis=1)
    parent_rows = picked * (inside * live_mid)[None, :]
    parent_cols = lax.all_to_all(parent_rows, "tile", split_axis=1, concat_axis=0, tiled=True)
    mid_block = (jnp.take(parent_cols, mid_list, axis=0) * live_mid[:, None]).T
    own_factor = factor_mid[0]
    cross_zero = jnp.zeros((rr_share, supernode), jnp.float32)
    mid_cross = apply_factor(
        mid_block, cross_zero, lax.all_gather(own_factor, "tile", axis=0, tiled=True)
    )
    factor_cols = lax.all_to_all(own_factor, "tile", split_axis=1, concat_axis=0, tiled=True)
    shard_piece = lax.all_gather(mid_cross, "tile", axis=0, tiled=True)
    running = dinv_mid[0]
    running = running - inner_rows(factor_cols, shard_piece)
    column = lax.dynamic_slice_in_dim(shard_piece, position * kk_share, kk_share, 1)
    crossed = column.T
    own_square = lax.dynamic_slice_in_dim(running, position * kk_share, kk_share, 1)
    variance_mid = jnp.diagonal(own_square)[None, :]
    kk_rows = jnp.concatenate([running, crossed], axis=1)
    rr_rows = jnp.concatenate([mid_cross, mid_block], axis=1)
    low_kk = jnp.take(kk_rows, low_list, axis=1) * live_low[None, :]
    low_rr = jnp.take(rr_rows, low_list, axis=1) * live_low[None, :]
    gathered_kk, gathered_rr = (
        lax.all_to_all(low_kk, "tile", split_axis=1, concat_axis=0, tiled=True),
        lax.all_to_all(low_rr, "tile", split_axis=1, concat_axis=0, tiled=True),
    )
    low_cols = jnp.concatenate([gathered_kk, gathered_rr], axis=0)
    low_block = (jnp.take(low_cols, low_list, axis=0) * live_low[:, None]).T
    lower_factor = factor_low[0]
    low_cross = apply_factor(
        low_block, cross_zero, lax.all_gather(lower_factor, "tile", axis=0, tiled=True)
    )
    partial_terms = jnp.sum(lower_factor * low_cross, axis=0)
    variance_low = diag_low[0] - lax.psum_scatter(
        partial_terms, "tile", scatter_dimension=0, tiled=True
    )
    return (variance_mid, variance_low[None, :])


def solution(mesh):
    return jax.shard_map(
        body,
        mesh=mesh,
        in_specs=(
            P(None, "tile", "leaf"),
            P("leaf"),
            P("leaf", None),
            P("leaf", None),
            P("leaf", None),
            P("leaf", "tile", None),
            P("leaf", "tile", None),
            P("leaf", "tile", None),
            P("leaf", "tile"),
        ),
        out_specs=(P("leaf", "tile"), P("leaf", "tile")),
        check_vma=False,
    )
```

profile of v0, /device:TPU:1, one launch (start us, length us, event | category | flops | bytes accessed | tf_op | source)
XLA Modules:
  0.0 300.0 jit_solution(1561551389065624958)
XLA Ops:
  7.2 0.0 all-gather.7.cloned.1.call-start
  7.2 0.7 all-gather.7.cloned.1.call-update
  7.9 0.0 all-gather.11.cloned.1.call-start
  7.9 0.7 all-gather.11.cloned.1.call-update
  9.3 1.3 fusion.34
  10.6 1.3 fusion.29
  12.0 0.1 mul.56
  12.0 0.7 fusion.33
  12.8 0.1 min.16
  12.8 0.7 fusion.27
  13.6 87.5 %all-gather.7.cloned.1.call-done = f32[4,128,2048]{1,2,0:T(8,128)} async-done(((f32[4,128,64]{1,2,0:T(8,128)}), f32[4,128,2048]{1,2,0:T(8,128)}) %all-gather.7.cloned.1.call-update) | async-done | bytes 4194320 | tf_op jit(solution)/shard_map/all_gather | solution.py:49
  101.1 1.3 dynamic-slice_bitcast_fusion
  102.4 2.6 gather_fusion
  105.0 1.3 select_multiply_fusion.4
  106.3 10.6 %all-to-all-start = ((f32[128,16,96]{0,2,1:T(8,128)}), f32[128,16,96]{0,2,1:T(8,128)S(1)}, u32[]{:S(2)}, u32[]{:S(2)}) async-start(f32[128,16,96]{0,2,1:T(8,128)} %select_multiply_fusion.4), calls=%async_computation | async-start | bytes 1572864 | tf_op jit(solution)/shard_map/all_to_all | solution.py:55
  116.9 0.0 all-gather.9.cloned.1.call-start
  117.0 0.6 fusion.25
  117.6 29.2 %all-to-all-done = f32[128,16,96]{0,2,1:T(8,128)S(1)} async-done(((f32[128,16,96]{0,2,1:T(8,128)}), f32[128,16,96]{0,2,1:T(8,128)S(1)}, u32[]{:S(2)}, u32[]{:S(2)}) %all-to-all-start) | async-done | bytes 786464 | tf_op jit(solution)/shard_map/all_to_all | solution.py:55
  146.8 0.3 copy.52
  147.2 2.6 gather_fusion.4
  149.8 0.0 copy-start.1
  149.8 0.0 copy-start.3
  149.8 10.3 %all-gather.11.cloned.1.call-done = f32[1,1536,512]{2,1,0:T(8,128)} async-done(((f32[1,96,512]{2,1,0:T(8,128)}), f32[1,1536,512]{2,1,0:T(8,128)}) %all-gather.11.cloned.1.call-update) | async-done | bytes 3145744 | tf_op jit(solution)/shard_map/all_gather | solution.py:60
  160.1 4.8 %fusion.5 = f32[96,512]{1,0:T(8,128)} fusion(f32[1,1536,512]{2,1,0:T(8,128)} %all-gather.11.cloned.1.call-done, f32[1536,96]{1,0:T(8,128)S(1)} %gather_fusion.4, f32[1536]{0:T(1024)S(1)} %get-tuple-element.7, pred[1536]{0:T(1024)(128)(4,1)S(1)} %get-tuple-element.8), kind=kOutput, calls=%fused_computation.12 | convolution fusion | flops 906313728 | bytes 3939840 | tf_op jit(solution)/shard_map/dot_general | solution.py:10
  165.0 0.0 all-gather.9.cloned.1.call-update
  165.0 0.0 all-gather.13.cloned.1.call-start
  165.0 0.5 all-gather.13.cloned.1.call-update
  165.6 0.8 copy.53
  166.4 4.4 %all-to-all-start.1 = ((f32[96,16,32]{0,2,1:T(8,128)}), f32[96,16,32]{0,2,1:T(8,128)S(1)}, u32[]{:S(2)}, u32[]{:S(2)}) async-start(f32[96,16,32]{0,2,1:T(8,128)} %bitcast.10), calls=%async_computation.1 | async-start | bytes 524288 | tf_op jit(solution)/shard_map/all_to_all | solution.py:62
  170.9 0.1 squeeze.43
  171.0 0.7 fusion.26
  171.7 0.7 fusion.24
  172.3 1.0 copy.57
  173.4 1.1 fusion.17
  174.5 0.1 pad_maximum_fusion.1
  174.6 0.0 copy-start.2
  174.6 2.6 gather_fusion.3
  177.2 1.3 select_multiply_fusion.3
  178.5 4.7 %all-to-all-done.1 = f32[96,16,32]{0,2,1:T(8,128)S(1)} async-done(((f32[96,16,32]{0,2,1:T(8,128)}), f32[96,16,32]{0,2,1:T(8,128)S(1)}, u32[]{:S(2)}, u32[]{:S(2)}) %all-to-all-start.1) | async-done | bytes 196640 | tf_op jit(solution)/shard_map/all_to_all | solution.py:62
  183.2 3.5 %all-to-all-start.3 = ((f32[96,16,96]{0,2,1:T(8,128)}), f32[96,16,96]{0,2,1:T(8,128)S(1)}, u32[]{:S(2)}, u32[]{:S(2)}) async-start(f32[96,16,96]{0,2,1:T(8,128)} %select_multiply_fusion.3), calls=%async_computation.3 | async-start | bytes 1572864 | tf_op jit(solution)/shard_map/all_to_all | solution.py:76
  186.8 0.1 copy.51
  186.9 0.2 copy.54
  187.1 0.1 all_to_all.56
  187.2 31.6 %all-gather.9.cloned.1.call-done = f32[1536,512]{1,0:T(8,128)} async-done(((f32[96,512]{1,0:T(8,128)}), f32[1536,512]{1,0:T(8,128)}) %all-gather.9.cloned.1.call-update) | async-done | bytes 3145744 | tf_op jit(solution)/shard_map/all_gather | solution.py:63
  218.8 1.4 dynamic-slice_bitcast_fusion.1
  220.2 6.9 %fusion.4 = f32[32,512]{0,1:T(8,128)S(1)} fusion(f32[1536,512]{1,0:T(8,128)} %all-gather.9.cloned.1.call-done, f32[1536,32]{0,1:T(8,128)S(1)} %all_to_all.56, f32[1,32,512]{1,2,0:T(8,128)S(1)} %copy.51), kind=kOutput, calls=%fused_computation.11 | convolution fusion | flops 302006272 | bytes 3473408 | tf_op jit(solution)/shard_map/dot_general | solution.py:14
  227.2 0.1 pad_maximum_fusion
  227.2 2.6 gather_fusion.2
  229.8 0.2 copy.56
  230.1 0.7 select_multiply_fusion.6
  230.8 0.0 all-to-all-done.3
  230.8 4.2 %all-to-all-start.2 = ((f32[32,16,96]{2,0,1:T(8,128)}), f32[32,16,96]{2,0,1:T(8,128)S(1)}, u32[]{:S(2)}, u32[]{:S(2)}) async-start(f32[32,16,96]{2,0,1:T(8,128)} %select_multiply_fusion.6), calls=%async_computation.2 | async-start | bytes 524288 | tf_op jit(solution)/shard_map/all_to_all | solution.py:75
  235.0 1.3 dynamic-slice
  237.0 0.3 copy.58
  237.3 1.2 gather_fusion.1
  238.5 9.6 %all-to-all-done.2 = f32[32,16,96]{2,0,1:T(8,128)S(1)} async-done(((f32[32,16,96]{2,0,1:T(8,128)}), f32[32,16,96]{2,0,1:T(8,128)S(1)}, u32[]{:S(2)}, u32[]{:S(2)}) %all-to-all-start.2) | async-done | bytes 196640 | tf_op jit(solution)/shard_map/all_to_all | solution.py:75
  248.0 0.1 pad_maximum_fusion.2
  248.1 0.0 copy-start
  248.1 2.6 gather_fusion.5
  250.7 0.0 copy-start.4
  250.7 14.8 %all-gather.13.cloned.1.call-done = f32[1,1536,512]{2,1,0:T(8,128)} async-done(((f32[1,96,512]{2,1,0:T(8,128)}), f32[1,1536,512]{2,1,0:T(8,128)}) %all-gather.13.cloned.1.call-update) | async-done | bytes 3145744 | tf_op jit(solution)/shard_map/all_gather | solution.py:82
  265.6 4.2 %fusion.14 = f32[512]{0:T(512)S(1)} fusion(f32[1,1536,512]{2,1,0:T(8,128)} %all-gather.13.cloned.1.call-done, f32[1536,96]{1,0:T(8,128)S(1)} %gather_fusion.5, f32[1536]{0:T(1024)S(1)} %fusion.26, pred[1536]{0:T(1024)(128)(4,1)S(1)} %compare_and_fusion, f32[1,96,512]{2,1,0:T(8,128)S(1)} %copy-done), kind=kOutput, calls=%fused_computation.15 | convolution fusion | flops 906411520 | bytes 3941888 | tf_op jit(solution)/shard_map/dot_general | solution.py:10
  269.8 23.2 %all-reduce = f32[512]{0:T(512)S(1)} all-reduce(f32[512]{0:T(512)S(1)} %fusion.14), channel_id=4, replica_groups=mesh['leaf'=32,'tile'=16] {'tile'}, use_global_device_ids=true, to_apply=%region_1.3.clone | all-reduce | flops 512 | bytes 4096
  292.9 0.6 fusion.30
  (17 shorter events, 0.1 us)
Async XLA Ops:
  7.2 93.9 %all-gather.7.cloned.1.call-start = ((), (), s32[]{:S(2)}) async-start(), calls=%async_computation.4 | async-start | bytes 4325376 | tf_op jit(solution)/shard_map/all_gather | solution.py:49
  7.9 152.2 %all-gather.11.cloned.1.call-start = ((), (), s32[]{:S(2)}) async-start(), calls=%async_computation.6 | async-start | bytes 3342336 | tf_op jit(solution)/shard_map/all_gather | solution.py:60
  106.3 40.5 %all-to-all-start = ((f32[128,16,96]{0,2,1:T(8,128)}), f32[128,16,96]{0,2,1:T(8,128)S(1)}, u32[]{:S(2)}, u32[]{:S(2)}) async-start(f32[128,16,96]{0,2,1:T(8,128)} %select_multiply_fusion.4), calls=%async_computation | async-start | bytes 1572864 | tf_op jit(solution)/shard_map/all_to_all | solution.py:55
  116.9 101.9 %all-gather.9.cloned.1.call-start = ((), (), s32[]{:S(2)}) async-start(), calls=%async_computation.5 | async-start | bytes 3342336 | tf_op jit(solution)/shard_map/all_gather | solution.py:63
  149.8 15.8 %copy-start.1 = (f32[1,96,512]{2,1,0:T(8,128)S(1)}, f32[1,96,512]{2,1,0:T(8,128)}, u32[]{:S(2)}) copy-start(f32[1,96,512]{2,1,0:T(8,128)} %param.16) | copy-start | bytes 589828
  149.8 21.1 %copy-start.3 = (s32[1,1536]{1,0:T(1,128)S(1)}, s32[1,1536]{1,0:T(1,128)}, u32[]{:S(2)}) copy-start(s32[1,1536]{1,0:T(1,128)} %param.15) | copy-start | bytes 18436
  165.0 100.6 %all-gather.13.cloned.1.call-start = ((), (), s32[]{:S(2)}) async-start(), calls=%async_computation.7 | async-start | bytes 3342336 | tf_op jit(solution)/shard_map/all_gather | solution.py:82
  166.4 16.8 %all-to-all-start.1 = ((f32[96,16,32]{0,2,1:T(8,128)}), f32[96,16,32]{0,2,1:T(8,128)S(1)}, u32[]{:S(2)}, u32[]{:S(2)}) async-start(f32[96,16,32]{0,2,1:T(8,128)} %bitcast.10), calls=%async_computation.1 | async-start | bytes 524288 | tf_op jit(solution)/shard_map/all_to_all | solution.py:62
  174.6 12.2 %copy-start.2 = (f32[1,32,512]{2,1,0:T(8,128)S(1)}, f32[1,32,512]{2,1,0:T(8,128)}, u32[]{:S(2)}) copy-start(f32[1,32,512]{2,1,0:T(8,128)} %param.17) | copy-start | bytes 196612
  183.2 47.6 %all-to-all-start.3 = ((f32[96,16,96]{0,2,1:T(8,128)}), f32[96,16,96]{0,2,1:T(8,128)S(1)}, u32[]{:S(2)}, u32[]{:S(2)}) async-start(f32[96,16,96]{0,2,1:T(8,128)} %select_multiply_fusion.3), calls=%async_computation.3 | async-start | bytes 1572864 | tf_op jit(solution)/shard_map/all_to_all | solution.py:76
  230.8 17.2 %all-to-all-start.2 = ((f32[32,16,96]{2,0,1:T(8,128)}), f32[32,16,96]{2,0,1:T(8,128)S(1)}, u32[]{:S(2)}, u32[]{:S(2)}) async-start(f32[32,16,96]{2,0,1:T(8,128)} %select_multiply_fusion.6), calls=%async_computation.2 | async-start | bytes 524288 | tf_op jit(solution)/shard_map/all_to_all | solution.py:75
  248.1 17.5 %copy-start = (f32[1,96,512]{2,1,0:T(8,128)S(1)}, f32[1,96,512]{2,1,0:T(8,128)}, u32[]{:S(2)}) copy-start(f32[1,96,512]{2,1,0:T(8,128)} %param.18) | copy-start | bytes 589828
  250.7 42.2 %copy-start.4 = (f32[1,32]{1,0:T(1,128)S(1)}, f32[1,32]{1,0:T(1,128)}, u32[]{:S(2)}) copy-start(f32[1,32]{1,0:T(1,128)} %param.19) | copy-start | bytes 388
Sparse Core Ops, SparseCore 0:
  11.2 89.8 all-gather.6
  103.2 56.8 all-gather.10
  165.1 53.6 all-gather.8
  220.8 44.7 all-gather.12
where the time goes:
time: 302 us; the launch traced here: 300 us
  waiting for transfers between devices  190 us (63%)
  blocking collectives  23.2 us (8%)
  local copies, waits for them, and re-layouts  22.9 us (8%)
  starting transfers between devices  22.8 us (8%)
  matrix products  15.9 us (5%)
  between operations  15.4 us (5%)
  other arithmetic  10.1 us (3%)
    all_gather x1, waiting for transfers between devices, body(): lax.all_gather(parent_cov, 'leaf', axis=2, tiled=True)  87.5 us
    all_gather x1, waiting for transfers between devices, body(): shard_piece = lax.all_gather(mid_cross, 'tile', axis=0, tiled=True)  31.6 us
    all_to_all x1, waiting for transfers between devices, body(): lax.all_to_all(parent_rows, 'tile', split_axis=1, concat_axis=0, tiled=True)  29.2 us
    unnamed x1, blocking collectives  23.2 us
    all_gather x1, waiting for transfers between devices, body(): lax.all_gather(lower_factor, 'tile', axis=0, tiled=True)  14.8 us
    all_to_all x1, starting transfers between devices, body(): lax.all_to_all(parent_rows, 'tile', split_axis=1, concat_axis=0, tiled=True)  10.6 us
    all_gather x1, waiting for transfers between devices, body(): lax.all_gather(own_factor, 'tile', axis=0, tiled=True)  10.3 us
    all_to_all x1, waiting for transfers between devices, body(): lax.all_to_all(low_kk, 'tile', split_axis=1, concat_axis=0, tiled=True)  9.56 us
  transfers between devices with their start and end apart: 8, of which 7 were waited for; matrix products, arithmetic and copies ran while one was open for 13% of the time, Pallas kernels for 0%

commit v1 on v0

v1 whole, which is shorter than its diff:
```python
import jax
import jax.numpy as jnp
from jax import lax
from jax.experimental import pallas as pl
from jax.experimental.pallas import tpu as pltpu
from jax.sharding import PartitionSpec as P

NX, NY, NZ, NC = 4, 8, 8, 2
NT = NZ * NC
S, M, F = 512, 1536, 2048
RB = F // NT
RF = M // NT
RK = S // NT
HB = RB // 2
CB = F // (NX * NY)
WIN, BLK = 768, 256
NB = M // BLK
BF, F32 = jnp.bfloat16, jnp.float32
MESH = pl.DeviceIdType.MESH

TOP, BOT, DI, ID, TOPL, BOTL, DIL, ROWS = 0, RB, 2 * RB, 2 * RB + RK, 2 * RB + 2 * RK, 3 * RB + 2 * RK, 4 * RB + 2 * RK, 4 * RB + 3 * RK


def split(v):
    hi = v.astype(BF)
    return hi, (v - hi.astype(F32)).astype(BF)


def dot(a, b):
    return jnp.dot(a, b, preferred_element_type=F32)


def kernel(
    cov, pmap, counts, rows_mid, rows_low, fm, dinv, fl, dlow,
    out_mid, out_low,
    ygath, stage, covsel, pmbuf, xm, xl, qoh, roh, csrc, u, v, fhi, flo, fin,
    y_send, y_recv, x_send, x_recv, p_send, p_recv, z_send, z_recv, c_send, c_recv, f_send, f_recv, l_sem,
):
    leaf, tile = lax.axis_index("leaf"), lax.axis_index("tile")
    x, y = leaf // NY, leaf % NY
    z, c = tile // NC, tile % NC

    def leaf_at(dx, dy):
        return lax.rem(x + dx + NX, NX) * NY + lax.rem(y + dy + NY, NY)

    def zt(dz, core=None):
        return lax.rem(z + dz + NZ, NZ) * NC + (c if core is None else core)

    sibling = z * NC + (1 - c)
    up, down = zt(1), zt(-1)
    ynext, yprev = leaf_at(0, 1), leaf_at(0, -1)

    barrier = pltpu.get_barrier_semaphore()
    for d in range(1, NT):
        pl.semaphore_signal(barrier, inc=1, device_id=(leaf, lax.rem(tile + d, NT)), device_id_type=MESH)
    for other in (ynext, yprev, leaf_at(1, 0), leaf_at(2, 0), leaf_at(3, 0)):
        pl.semaphore_signal(barrier, inc=1, device_id=(other, tile), device_id_type=MESH)

    for p in range(4):
        ygath[y, p] = jnp.concatenate([cov[p, :HB, :], cov[p, HB:, :]], axis=1)
    pmbuf[x] = jnp.full((8, 128), pmap[0], jnp.int32)
    pl.semaphore_wait(barrier, NT - 1 + 5)

    def send(src, dst, ssem, rsem, where):
        pltpu.make_async_remote_copy(
            src_ref=src, dst_ref=dst, send_sem=ssem, recv_sem=rsem, device_id=where, device_id_type=MESH
        ).start()

    def wait(ref, sem):
        pltpu.make_async_copy(ref, ref, sem).wait()

    for dx in (1, 2, 3):
        send(pmbuf.at[x], pmbuf.at[x], p_send, p_recv, (leaf_at(dx, 0), tile))
    send(ygath.at[y], ygath.at[y], y_send, y_recv.at[0, 0], (ynext, tile))
    send(ygath.at[y], ygath.at[y], y_send, y_recv.at[1, 0], (yprev, tile))
    facs = ((fm, xm), (fl, xl))
    for a, (own, whole) in enumerate(facs):
        send(own, whole.at[tile], z_send.at[a], z_recv.at[a, 0, 0], (leaf, up))
        send(own, whole.at[tile], z_send.at[a], z_recv.at[a, 1, 0], (leaf, down))
        send(own, whole.at[tile], c_send.at[a], c_recv.at[a], (leaf, sibling))
        pltpu.make_async_copy(own, whole.at[tile], l_sem.at[a]).start()

    live_mid, live_low = counts[0, 0], counts[0, 1]
    lane = lax.broadcasted_iota(jnp.int32, (1, M), 1)
    midv = jnp.where(lane < live_mid, rows_mid[...], -1)
    lowv = jnp.where(lane < live_low, rows_low[...], -1)
    for b in range(NB):
        cols = slice(b * BLK, (b + 1) * BLK)
        pos = lax.broadcasted_iota(jnp.int32, (WIN, BLK), 0) + b * BLK
        qoh[b] = (pos == midv[:, cols]).astype(F32).astype(BF)
        roh[b] = (pos == lowv[:, cols]).astype(F32).astype(BF)
    u[BOT : BOT + RB, S:] = (lax.broadcasted_iota(jnp.int32, (RB, M), 0) + tile * RB == midv).astype(F32).astype(BF)
    dhi, dlo = split(dinv[...])
    eye = lax.broadcasted_iota(jnp.int32, (RK, S), 0) + tile * RK == lax.broadcasted_iota(jnp.int32, (RK, S), 1)
    u[DI : DI + RK, :S] = dhi
    u[ID : ID + RK, :S] = eye.astype(F32).astype(BF)
    u[DIL : DIL + RK, :S] = dlo
    for r0, n in ((DI, 2 * RK), (BOTL, RB + RK)):
        u[r0 : r0 + n, S : 2 * S] = jnp.zeros((n, S), BF)

    wait(pmbuf.at[pl.ds(0, 3)], p_recv)

    def choose(ys):
        for dx in range(NX):
            pm = jnp.broadcast_to(pmbuf[lax.rem(x + dx, NX)][0:1], (HB, 128))
            got = jnp.where(
                pm < 2,
                jnp.where(pm == 0, ygath[ys, 0], ygath[ys, 1]),
                jnp.where(pm == 2, ygath[ys, 2], ygath[ys, 3]),
            )
            if dx == 0:
                covsel[x * NY + ys] = got
            else:
                stage[dx - 1, ys] = got
                send(stage.at[dx - 1, ys], covsel.at[x * NY + ys], x_send, x_recv, (leaf_at(dx, 0), tile))

    choose(y)
    HR = RF // 2
    for s in range(1, 5):
        yb, ya = lax.rem(y + NY - s, NY), lax.rem(y + s, NY)
        if s < 4:
            wait(ygath.at[yb], y_recv.at[0, s - 1])
            wait(ygath.at[ya], y_recv.at[1, s - 1])
            if s < 3:
                send(ygath.at[yb], ygath.at[yb], y_send, y_recv.at[0, s], (ynext, tile))
                send(ygath.at[ya], ygath.at[ya], y_send, y_recv.at[1, s], (yprev, tile))
            else:
                lo, hi = pl.ds(0, 2), pl.ds(2, 2)
                send(ygath.at[yb, lo], ygath.at[yb, lo], y_send, y_recv.at[0, s], (ynext, tile))
                send(ygath.at[ya, hi], ygath.at[ya, hi], y_send, y_recv.at[1, s], (yprev, tile))
            choose(yb)
            choose(ya)
        else:
            wait(ygath.at[yb, pl.ds(0, 2)], y_recv.at[0, s - 1])
            wait(ygath.at[yb, pl.ds(2, 2)], y_recv.at[1, s - 1])
            choose(yb)
        for a, (_, whole) in enumerate(facs):
            tb, ta = zt(-s), zt(s)
            if s < 4:
                wait(whole.at[tb], z_recv.at[a, 0, s - 1])
                wait(whole.at[ta], z_recv.at[a, 1, s - 1])
                if s < 3:
                    send(whole.at[tb], whole.at[tb], z_send.at[a], z_recv.at[a, 0, s], (leaf, up))
                    send(whole.at[ta], whole.at[ta], z_send.at[a], z_recv.at[a, 1, s], (leaf, down))
                else:
                    lo, hi = pl.ds(0, HR), pl.ds(HR, HR)
                    send(whole.at[tb, lo], whole.at[tb, lo], z_send.at[a], z_recv.at[a, 0, s], (leaf, up))
                    send(whole.at[ta, hi], whole.at[ta, hi], z_send.at[a], z_recv.at[a, 1, s], (leaf, down))
                send(whole.at[tb], whole.at[tb], c_send.at[a], c_recv.at[a], (leaf, sibling))
                send(whole.at[ta], whole.at[ta], c_send.at[a], c_recv.at[a], (leaf, sibling))
            else:
                wait(whole.at[tb, pl.ds(0, HR)], z_recv.at[a, 0, s - 1])
                wait(whole.at[tb, pl.ds(HR, HR)], z_recv.at[a, 1, s - 1])
                send(whole.at[tb], whole.at[tb], c_send.at[a], c_recv.at[a], (leaf, sibling))

    wait(covsel.at[pl.ds(0, (NX - 1) * NY)], x_recv)
    low_half = lax.broadcasted_iota(jnp.int32, (HB, 128), 1) < CB
    for m in range(F // 128):
        a, b = covsel[2 * m], covsel[2 * m + 1]
        ra, rb = pltpu.roll(a, CB, 1), pltpu.roll(b, CB, 1)
        for r0, val in ((0, jnp.where(low_half, a, rb)), (HB, jnp.where(low_half, ra, b))):
            hi, lo = split(val)
            csrc[r0 : r0 + HB, m * 128 : (m + 1) * 128] = hi
            csrc[RB + r0 : RB + r0 + HB, m * 128 : (m + 1) * 128] = lo
    for b in range(NB):
        got = dot(csrc[:, b * BLK : b * BLK + WIN], qoh[b]).astype(BF)
        u[TOP : TOP + RB, S + b * BLK : S + (b + 1) * BLK] = got[:RB]
        u[TOPL : TOPL + RB, S + b * BLK : S + (b + 1) * BLK] = got[RB:]

    def pick(r0, n, b):
        cols = slice(b * BLK, (b + 1) * BLK)
        v[r0 : r0 + n, cols] = dot(u[r0 : r0 + n, b * BLK : b * BLK + WIN], roh[b]).astype(BF)

    for b in range(2, NB):
        pick(TOP, 2 * RB, b)
        pick(TOPL, RB, b)

    def halves(a, whole):
        wait(whole.at[tile], l_sem.at[a])
        wait(whole.at[pl.ds(0, NZ)], c_recv.at[a])
        for t in range(NT):
            hi, lo = split(whole[t])
            fhi[t * RF : (t + 1) * RF] = hi
            flo[t * RF : (t + 1) * RF] = lo

    halves(0, xm)
    both = dot(u[TOP : TOP + 2 * RB, S:], fhi[...]) + dot(u[TOP : TOP + 2 * RB, S:], flo[...])
    cross = both[:RB] + dot(u[TOPL : TOPL + RB, S:], fhi[...])
    own = both[RB:]
    part_mid = jnp.sum(cross * own, axis=0, keepdims=True) + jnp.sum(jnp.where(eye, dinv[...], 0.0), axis=0, keepdims=True)
    for r0, rl, val in ((TOP, TOPL, cross), (BOT, BOTL, own)):
        hi, lo = split(-val)
        u[r0 : r0 + RB, :S] = hi
        u[rl : rl + RB, :S] = lo
    for b in range(2):
        pick(0, ROWS, b)

    halves(1, xl)
    H = TOPL
    early = dot(v[:, :S], fhi[:S])
    low = dot(v[:H, :S], flo[:S])
    tall = dot(v[: 2 * RB, S:], fhi[S:]) + dot(v[: 2 * RB, S:], flo[S:])
    tail = dot(v[TOPL : TOPL + RB, S:], fhi[S:])
    front = early[:H] + low
    top = front[:RB] + early[TOPL : TOPL + RB] + tall[:RB] + tail
    bot = front[BOT : BOT + RB] + early[BOTL : BOTL + RB] + tall[RB:]
    kk = front[DI : DI + RK] + early[DIL : DIL + RK]
    part_low = jnp.sum(top * bot, axis=0, keepdims=True) + jnp.sum(kk * front[ID : ID + RK], axis=0, keepdims=True)

    for k in range(4):
        fin[tile, k : k + 1] = part_mid[:, k * 128 : (k + 1) * 128]
        fin[tile, k + 4 : k + 5] = part_low[:, k * 128 : (k + 1) * 128]
    for d in range(1, NT):
        send(fin.at[tile], fin.at[tile], f_send, f_recv, (leaf, lax.rem(tile + d, NT)))
    wait(fin.at[pl.ds(0, NT - 1)], f_recv)
    total = jnp.sum(fin[...], axis=0)
    per = 128 // RK
    row = lax.broadcasted_iota(jnp.int32, (8, 128), 0)
    turn = lax.rem(128 - lax.rem(tile, per) * RK, 128)
    for out, base, add in ((out_mid, 0, None), (out_low, 4, dlow)):
        line = jnp.sum(jnp.where(row == base + tile // per, total, 0.0), axis=0, keepdims=True)
        line = pltpu.roll(jnp.broadcast_to(line, (8, 128)), turn, 1)[0:1, :RK]
        out[...] = line if add is None else line + add[...]

    wait(fin.at[pl.ds(0, NT - 1)], f_send)
    wait(pmbuf.at[pl.ds(0, 3)], p_send)
    wait(ygath.at[pl.ds(0, NY - 1)], y_send)
    wait(stage, x_send)
    for a, (_, whole) in enumerate(facs):
        wait(whole.at[pl.ds(0, NZ - 1)], z_send.at[a])
        wait(whole.at[pl.ds(0, NZ)], c_send.at[a])


def body(parent_cov, parent_map, front_rows, rows_mid, rows_low, factor_mid, dinv_mid, factor_low, diag_low):
    vm, sm = pl.BlockSpec(memory_space=pltpu.VMEM), pl.BlockSpec(memory_space=pltpu.SMEM)
    dma = pltpu.SemaphoreType.DMA
    return pl.pallas_call(
        kernel,
        out_shape=[jax.ShapeDtypeStruct((1, RK), F32)] * 2,
        in_specs=[vm, sm, sm, vm, vm, vm, vm, vm, vm],
        out_specs=[vm, vm],
        scratch_shapes=[
            pltpu.VMEM((NY, 4, HB, 128), F32),
            pltpu.VMEM((NX - 1, NY, HB, 128), F32),
            pltpu.VMEM((NX * NY, HB, 128), F32),
            pltpu.VMEM((NX, 8, 128), jnp.int32),
            pltpu.VMEM((NT, RF, S), F32),
            pltpu.VMEM((NT, RF, S), F32),
            pltpu.VMEM((NB, WIN, BLK), BF),
            pltpu.VMEM((NB, WIN, BLK), BF),
            pltpu.VMEM((2 * RB, F), BF),
            pltpu.VMEM((ROWS, F), BF),
            pltpu.VMEM((ROWS, M), BF),
            pltpu.VMEM((M, S), BF),
            pltpu.VMEM((M, S), BF),
            pltpu.VMEM((NT, 8, 128), F32),
            dma, dma((2, 4)), dma, dma, dma, dma, dma((2,)), dma((2, 2, 4)), dma((2,)), dma((2,)), dma, dma, dma((2,)),
        ],
        compiler_params=pltpu.CompilerParams(
            collective_id=0, has_side_effects=True, vmem_limit_bytes=48 * 1024 * 1024
        ),
        cost_estimate=pl.CostEstimate(flops=5 * 10**9, bytes_accessed=10**6, transcendentals=0),
    )(parent_cov, parent_map, front_rows, rows_mid, rows_low, factor_mid[0], dinv_mid[0], factor_low[0], diag_low)


def solution(mesh):
    return jax.shard_map(
        body,
        mesh=mesh,
        in_specs=(
            P(None, "tile", "leaf"),
            P("leaf"),
            P("leaf", None),
            P("leaf", None),
            P("leaf", None),
            P("leaf", "tile", None),
            P("leaf", "tile", None),
            P("leaf", "tile", None),
            P("leaf", "tile"),
        ),
        out_specs=(P("leaf", "tile"), P("leaf", "tile")),
        check_vma=False,
    )
```

time: 302 us -> 62.4 us (0.21)
  waiting for transfers between devices: 190 us -> 0 us
  Pallas kernels: 0 us -> 56.5 us
  blocking collectives: 23.2 us -> 0 us
  starting transfers between devices: 22.8 us -> 0 us
  local copies, waits for them, and re-layouts: 22.9 us -> 4.34 us
  matrix products: 15.9 us -> 0 us
  between operations: 15.4 us -> 1.37 us
  other arithmetic: 10.1 us -> 0 us
    all_gather x4 -> x0, waiting for transfers between devices: 144 us -> none  [the longest x1 87.5 us: body(): lax.all_gather(parent_cov, 'leaf', axis=2, tiled=True)]
    pallas_call x0 -> x1, Pallas kernels: none -> 56.5 us  [body(): pl.pallas_call(kernel, out_shape=[jax.ShapeDtypeStruct((1, RK), F32)] * 2...]
    all_to_all x4 -> x0, waiting for transfers between devices: 43.5 us -> none  [the longest x1 29.2 us: body(): lax.all_to_all(parent_rows, 'tile', split_axis=1, concat_axis=0, tiled=True)]
    unnamed x1 -> x0, blocking collectives: 23.2 us -> none
    all_to_all x4 -> x0, starting transfers between devices: 22.7 us -> none  [the longest x1 10.6 us: body(): lax.all_to_all(parent_rows, 'tile', split_axis=1, concat_axis=0, tiled=True)]
    dot_general x3 -> x0, matrix products: 15.9 us -> none  [the longest x2 9.02 us: matmul(): jnp.dot(left, right, precision=EXACT_PRECISION, preferred_element_type=jn...]
    gather x7 -> x0, local copies, waits for them, and re-layouts: 14.4 us -> none  [the longest x2 2.84 us: body(): low_kk = jnp.take(kk_rows, low_list, axis=1) * live_low[None, :]]
    mul x4 -> x0, other arithmetic: 4.72 us -> none  [the longest x2 2.67 us: body(): parent_rows = picked * (inside * live_mid)[None, :]]
  transfers between devices with their start and end apart: 8 -> 0, of which waited for: 7 -> 0; matrix products, arithmetic and copies ran while one was open for 13% -> 0% of each run, Pallas kernels for 0% -> 0%
where the time goes in v1:
time: 62.4 us; the launch traced here: 62.2 us
  Pallas kernels  56.5 us (91%)
  local copies, waits for them, and re-layouts  4.34 us (7%)
  between operations  1.37 us (2%)
    pallas_call x1, Pallas kernels, body(): pl.pallas_call(kernel, out_shape=[jax.ShapeDtypeStruct((1, RK), F32)] * 2...  56.5 us
    unnamed x17, local copies, waits for them, and re-layouts  4.34 us

profile of v1, /device:TPU:1, one launch (start us, length us, event | category | flops | bytes accessed | tf_op | source)
XLA Modules:
  0.0 62.2 jit_solution(3830797753235962351)
XLA Ops:
  1.3 0.0 copy-start.5
  1.3 0.0 copy-start.6
  1.3 0.0 copy-start
  1.3 0.0 copy-start.1
  1.3 1.1 %copy.11.cov = f32[4,128,64]{2,1,0:T(8,128)S(1)} copy(f32[4,128,64]{1,2,0:T(8,128)} %param.9) | data formatting | bytes 262144 | tf_op args[0]
  2.4 0.0 copy-done.5
  2.4 0.0 copy-done.6
  2.4 0.0 copy-done
  2.4 0.0 copy-done.1
  2.4 0.0 copy-start.2
  2.5 0.8 %copy-done.2 = f32[1,32,512]{2,1,0:T(8,128)S(1)} copy-done((f32[1,32,512]{2,1,0:T(8,128)S(1)}, f32[1,32,512]{2,1,0:T(8,128)}, u32[]{:S(2)}) %copy-start.2) | copy-done | bytes 65560
  3.3 0.0 copy-start.3
  3.3 0.7 %copy-done.3 = s32[1,1536]{1,0:T(1,128)S(1)} copy-done((s32[1,1536]{1,0:T(1,128)S(1)}, s32[1,1536]{1,0:T(1,128)}, u32[]{:S(2)}) %copy-start.3) | copy-done | bytes 6168
  4.0 0.0 copy-start.4
  4.0 0.7 %copy-done.4 = s32[1,1536]{1,0:T(1,128)S(1)} copy-done((s32[1,1536]{1,0:T(1,128)S(1)}, s32[1,1536]{1,0:T(1,128)}, u32[]{:S(2)}) %copy-start.4) | copy-done | bytes 6168
  4.7 56.5 %shard_map.104 = (f32[1,32]{1,0:T(1,128)S(1)}, f32[1,32]{1,0:T(1,128)S(1)}) custom-call(f32[4,128,64]{2,1,0:T(8,128)S(1)} %copy.11.cov, s32[1]{0:T(128)S(6)} %copy.14.pmap, s32[1,2]{1,0:T(1,128)S(1)} %copy-done.5, s32[1,1536]{1,0:T(1,128)S(1)} %copy-done.3, s32[1,1536]{1,0:T(1,128)S(1)} %copy-done.4, f32[96,512]{1,0:T(8,128)S(1)} %bitcast.3, ...), custom_call_target="tpu_custom_call" | custom-call | flops 5000000000 | bytes 1000000 | tf_op jit(solution)/shard_map/pallas_call | solution.py:237
  61.2 0.5 copy.15
  61.7 0.5 copy.16
Async XLA Ops:
  1.3 1.1 %copy-start.5 = (s32[1,2]{1,0:T(1,128)S(1)}, s32[1,2]{1,0:T(1,128)}, u32[]{:S(2)}) copy-start(s32[1,2]{1,0:T(1,128)} %counts.1) | copy-start | bytes 28
  1.3 1.1 %copy-start.6 = (f32[1,32]{1,0:T(1,128)S(1)}, f32[1,32]{1,0:T(1,128)}, u32[]{:S(2)}) copy-start(f32[1,32]{1,0:T(1,128)} %dlow.1) | copy-start | bytes 388
  1.3 1.1 %copy-start = (f32[1,96,512]{2,1,0:T(8,128)S(1)}, f32[1,96,512]{2,1,0:T(8,128)}, u32[]{:S(2)}) copy-start(f32[1,96,512]{2,1,0:T(8,128)} %param.14) | copy-start | bytes 589828
  1.3 1.1 %copy-start.1 = (f32[1,96,512]{2,1,0:T(8,128)S(1)}, f32[1,96,512]{2,1,0:T(8,128)}, u32[]{:S(2)}) copy-start(f32[1,96,512]{2,1,0:T(8,128)} %param.16) | copy-start | bytes 589828
  2.4 0.8 %copy-start.2 = (f32[1,32,512]{2,1,0:T(8,128)S(1)}, f32[1,32,512]{2,1,0:T(8,128)}, u32[]{:S(2)}) copy-start(f32[1,32,512]{2,1,0:T(8,128)} %param.15) | copy-start | bytes 196612
  3.3 0.7 %copy-start.3 = (s32[1,1536]{1,0:T(1,128)S(1)}, s32[1,1536]{1,0:T(1,128)}, u32[]{:S(2)}) copy-start(s32[1,1536]{1,0:T(1,128)} %rows_mid.1) | copy-start | bytes 18436
  4.0 0.7 %copy-start.4 = (s32[1,1536]{1,0:T(1,128)S(1)}, s32[1,1536]{1,0:T(1,128)}, u32[]{:S(2)}) copy-start(s32[1,1536]{1,0:T(1,128)} %rows_low.1) | copy-start | bytes 18436

commit v2 on v1

v2 whole, which is shorter than its diff:
```python
import jax
import jax.numpy as jnp
from jax import lax
from jax.experimental import pallas as pl
from jax.experimental.pallas import tpu as pltpu
from jax.sharding import PartitionSpec as P

NX, NY, NZ, NC = 4, 8, 8, 2
NT, NL = NZ * NC, NX * NY
NP, S, M, F = 4, 512, 1536, 2048
RB = F // NT
RF = M // NT
RK = S // NT
CB = F // NL
PL = NC * RF
WIN, BLK = 768, 256
NB = M // BLK
BF, F32, I32 = jnp.bfloat16, jnp.float32, jnp.int32
MESH = pl.DeviceIdType.MESH
AHEAD = 9

TOP, BOT, DI, ID, TOPL, BOTL, DIL, ROWS = 0, RB, 2 * RB, 2 * RB + RK, 2 * RB + 2 * RK, 3 * RB + 2 * RK, 4 * RB + 2 * RK, 4 * RB + 3 * RK


def ring_order():
    def pieces(a, s):
        if s < 3:
            return [(a, s, 0, 32), (a, s, 32, 32), (a, s, 64, 32)]
        return [(a, s, 0, 32), (a, s, 32, 16)]

    up = []
    for s in range(5):
        up += (pieces(0, s) if s < 4 else []) + (pieces(1, s - 1) if s > 0 else [])
    down = [(a, s, RF - r - n, n) for a, s, r, n in up]
    return up, down


UP, DOWN = ring_order()
NPIECE = len(UP)


def source_of(seq, k):
    a, s, r, n = seq[k]
    return next(i for i, (b, q, r0, m) in enumerate(seq) if b == a and q == s - 1 and r0 <= r and r + n <= r0 + m)


def split(v):
    hi = v.astype(BF)
    return hi, (v - hi.astype(F32)).astype(BF)


def dot(a, b):
    return jnp.dot(a, b, preferred_element_type=F32)


def kernel(
    pmap, counts, cov, rows_mid, rows_low, fm, dinv, fl, dlow,
    out_mid, out_low,
    ygath, stage, covsel, pmbuf, xm, xl, rbuf, dbuf, lbuf, qoh, roh, csrc, u, v, fhi, flo, yhi, ylo, fin,
    y_send, y_recv, x_send, x_recv, p_send, p_recv, z_send, z_recv, c_send, c_recv, f_send, f_recv, l_sem,
):
    leaf, tile = lax.axis_index("leaf"), lax.axis_index("tile")
    x, y = leaf // NY, leaf % NY
    z, c = tile // NC, tile % NC

    def leaf_at(dx, dy):
        return lax.rem(x + dx + NX, NX) * NY + lax.rem(y + dy + NY, NY)

    def zt(dz):
        return lax.rem(z + dz + NZ, NZ) * NC + c

    sibling = z * NC + (1 - c)
    up, down = zt(1), zt(-1)
    ynext, yprev = leaf_at(0, 1), leaf_at(0, -1)
    own, whole = (fm, fl), (xm, xl)

    barrier = pltpu.get_barrier_semaphore()
    near = [(leaf, up), (leaf, down), (leaf, sibling), (ynext, tile), (yprev, tile)]
    near += [(leaf_at(dx, 0), tile) for dx in (1, 2, 3)]
    for other in near:
        pl.semaphore_signal(barrier, inc=1, device_id=other, device_id_type=MESH)

    local = [
        (cov, ygath.at[y]), (rows_mid, rbuf.at[0:1]), (rows_low, rbuf.at[1:2]), (dinv, dbuf), (dlow, lbuf),
        (fm, xm.at[tile]), (fl, xl.at[tile]),
    ]
    local = [pltpu.make_async_copy(src, dst, l_sem.at[i]) for i, (src, dst) in enumerate(local)]
    for copy in local:
        copy.start()
    pmbuf[x] = jnp.full((8, 128), pmap[0], I32)
    pl.semaphore_wait(barrier, len(near))

    def send(src, dst, ssem, rsem, where):
        pltpu.make_async_remote_copy(
            src_ref=src, dst_ref=dst, send_sem=ssem, recv_sem=rsem, device_id=where, device_id_type=MESH
        ).start()

    def wait(ref, sem):
        pltpu.make_async_copy(ref, ref, sem).wait()

    def y_piece(d, j):
        s, p = divmod(j, NP)
        return s, (p if d == 0 else NP - 1 - p)

    def y_go(d, j):
        s, p = y_piece(d, j)
        src_y = lax.rem(y + (NY - s if d == 0 else s), NY)
        dst = ygath.at[src_y, p]
        send(cov.at[p] if s == 0 else dst, dst, y_send, y_recv.at[d, j], (ynext if d == 0 else yprev, tile))

    def y_come(d, j):
        s, p = y_piece(d, j)
        wait(ygath.at[lax.rem(y + (NY - 1 - s if d == 0 else s + 1), NY), p], y_recv.at[d, j])

    def z_go(d, k):
        a, s, r, n = (UP, DOWN)[d][k]
        dst = whole[a].at[zt(-s if d == 0 else s), pl.ds(r, n)]
        send(own[a].at[pl.ds(r, n)] if s == 0 else dst, dst, z_send, z_recv.at[d, k], (leaf, up if d == 0 else down))

    def z_come(d, k):
        a, s, r, n = (UP, DOWN)[d][k]
        wait(whole[a].at[zt(-s - 1 if d == 0 else s + 1), pl.ds(r, n)], z_recv.at[d, k])

    for dx in (1, 2, 3):
        send(pmbuf.at[x], pmbuf.at[x], p_send, p_recv, (leaf_at(dx, 0), tile))
    for j in range(NP):
        y_go(0, j)
        y_go(1, j)
    due = {}
    for d, seq in ((0, UP), (1, DOWN)):
        for k in range(NPIECE):
            after = k - AHEAD if seq[k][1] == 0 else max(k - AHEAD, source_of(seq, k))
            if after < 0:
                z_go(d, k)
            else:
                due.setdefault(after, []).append((d, k))
    for a in range(2):
        send(own[a], whole[a].at[tile], c_send, c_recv.at[a, 0], (leaf, sibling))

    for copy in local:
        copy.wait()
    live_mid, live_low = counts[0, 0], counts[0, 1]
    lane = lax.broadcasted_iota(I32, (1, M), 1)
    midv = jnp.where(lane < live_mid, rbuf[0:1], -1)
    lowv = jnp.where(lane < live_low, rbuf[1:2], -1)
    eye = lax.broadcasted_iota(I32, (RK, S), 0) + tile * RK == lax.broadcasted_iota(I32, (RK, S), 1)

    def mid_onehot(b):
        pos = lax.broadcasted_iota(I32, (WIN, BLK), 0) + b * BLK
        qoh[b] = (pos == midv[:, b * BLK : (b + 1) * BLK]).astype(F32).astype(BF)

    def low_start(p):
        return p * PL // 128 * 128

    def low_onehot(p):
        pos = lax.broadcasted_iota(I32, (WIN, PL), 0) + low_start(p)
        roh[p] = (pos == lowv[:, p * PL : (p + 1) * PL]).astype(F32).astype(BF)

    def rows_without_transfer():
        u[BOT : BOT + RB, S:] = (lax.broadcasted_iota(I32, (RB, M), 0) + tile * RB == midv).astype(F32).astype(BF)
        dhi, dlo = split(dbuf[...])
        u[DI : DI + RK, :S] = dhi
        u[ID : ID + RK, :S] = eye.astype(F32).astype(BF)
        u[DIL : DIL + RK, :S] = dlo
        for r0, n in ((DI, 2 * RK), (BOTL, RB + RK)):
            u[r0 : r0 + n, S:] = jnp.zeros((n, M), BF)

    def choose(ys):
        for dx in range(NX):
            pm = jnp.broadcast_to(pmbuf[lax.rem(x + dx, NX)][0:1], (CB, RB))
            got = jnp.where(
                pm < 2,
                jnp.where(pm == 0, ygath[ys, 0], ygath[ys, 1]),
                jnp.where(pm == 2, ygath[ys, 2], ygath[ys, 3]),
            )
            if dx == 0:
                covsel[x * NY + ys] = got
            else:
                stage[dx - 1, ys] = got
                send(stage.at[dx - 1, ys], covsel.at[x * NY + ys], x_send, x_recv, (leaf_at(dx, 0), tile))

    def pass_on(a, s):
        for t in (zt(-s), zt(s))[: 2 if s < 4 else 1]:
            send(whole[a].at[t], whole[a].at[t], c_send, c_recv.at[a, s], (leaf, sibling))

    def parent_columns():
        wait(covsel.at[pl.ds(0, (NX - 1) * NY)], x_recv)
        for m in range(F // 128):
            hi, lo = split(covsel[2 * m : 2 * m + 2].reshape(128, RB).T)
            csrc[:RB, m * 128 : (m + 1) * 128] = hi
            csrc[RB:, m * 128 : (m + 1) * 128] = lo
        for b in range(NB):
            got = dot(csrc[:, b * BLK : b * BLK + WIN], qoh[b]).astype(BF)
            u[TOP : TOP + RB, S + b * BLK : S + (b + 1) * BLK] = got[:RB]
            u[TOPL : TOPL + RB, S + b * BLK : S + (b + 1) * BLK] = got[RB:]

    def pick(p):
        v[p] = dot(u[:, low_start(p) : low_start(p) + WIN], roh[p]).astype(BF)

    def chip_rows(a, s):
        return (z,) if s == 0 else (lax.rem(z + s, NZ),) if s == 4 else (lax.rem(z + NZ - s, NZ), lax.rem(z + s, NZ))

    def come_from_sibling(a, s):
        wait(whole[a].at[pl.ds(0, 2 if 0 < s < 4 else 1)], c_recv.at[a, s])

    def mid_halves(s):
        come_from_sibling(0, s)
        for p in chip_rows(0, s):
            hi, lo = split(xm[pl.ds(p * NC, NC)].reshape(PL, S))
            fhi[pl.ds(p * PL, PL)] = hi
            flo[pl.ds(p * PL, PL)] = lo

    def low_terms(s):
        come_from_sibling(1, s)
        for p in chip_rows(1, s):
            hi, lo = split(xl[pl.ds(p * NC, NC)].reshape(PL, S))
            left = v[p]
            first, second = dot(left, hi), dot(left[:TOPL], lo)
            yhi[...] = first if s == 0 else yhi[...] + first
            ylo[...] = second if s == 0 else ylo[...] + second

    def cross_rows():
        both = dot(u[: 2 * RB, S:], fhi[...]) + dot(u[: 2 * RB, S:], flo[...])
        cross = both[:RB] + dot(u[TOPL : TOPL + RB, S:], fhi[...])
        mine = both[RB:]
        part = jnp.sum(cross * mine, axis=0, keepdims=True) + jnp.sum(jnp.where(eye, dbuf[...], 0.0), axis=0, keepdims=True)
        for k in range(4):
            fin[tile, k : k + 1] = part[:, k * 128 : (k + 1) * 128]
        for r0, rl, val in ((TOP, TOPL, cross), (BOT, BOTL, mine)):
            hi, lo = split(-val)
            u[r0 : r0 + RB, :S] = hi
            u[rl : rl + RB, :S] = lo

    rows_without_transfer()
    wait(pmbuf.at[pl.ds(0, 3)], p_recv)
    choose(y)

    beside = {}

    def at(k, f, *args):
        beside.setdefault(k, []).append((f, args))

    for b in range(NB):
        at(3 + b, mid_onehot, b)
    for p in range(NZ):
        at(4 + p, low_onehot, p)
    at(8, mid_halves, 0)
    at(9, mid_halves, 1)
    at(10, mid_halves, 2)
    at(12, parent_columns)
    for p in range(3, NZ):
        at(13, pick, p)
    at(14, mid_halves, 3)
    at(17, mid_halves, 4)
    at(17, cross_rows)
    for p in range(3):
        at(17, pick, p)
    for s in range(3):
        at(18, low_terms, s)
    at(19, low_terms, 3)
    at(21, low_terms, 4)

    ny = 3 * NP + NP // 2
    jy = 0
    for k in range(NPIECE):
        while jy < ny and jy <= 2 * k:
            for d in (0, 1):
                y_come(d, jy)
                if jy + NP < ny:
                    y_go(d, jy + NP)
            s, p = divmod(jy, NP)
            if s < 3 and p == NP - 1:
                choose(lax.rem(y + NY - 1 - s, NY))
                choose(lax.rem(y + s + 1, NY))
            elif jy == ny - 1:
                choose(lax.rem(y + NY // 2, NY))
            jy += 1
        z_come(0, k)
        z_come(1, k)
        for d, q in due.get(k, ()):
            z_go(d, q)
        a, s = UP[k][:2]
        if k + 1 == NPIECE or UP[k + 1][:2] != (a, s):
            pass_on(a, s + 1)
        for f, args in beside.get(k, ()):
            f(*args)

    def rows(r0, rl, n):
        return yhi[r0 : r0 + n] + yhi[rl : rl + n] + ylo[r0 : r0 + n]

    part = jnp.sum(rows(TOP, TOPL, RB) * rows(BOT, BOTL, RB), axis=0, keepdims=True)
    part += jnp.sum(rows(DI, DIL, RK) * (yhi[ID : ID + RK] + ylo[ID : ID + RK]), axis=0, keepdims=True)
    for k in range(4):
        fin[tile, k + 4 : k + 5] = part[:, k * 128 : (k + 1) * 128]

    for d in sorted(range(1, NT), key=lambda d: -min(d, NT - d)):
        send(fin.at[tile], fin.at[tile], f_send, f_recv, (leaf, lax.rem(tile + d, NT)))
    wait(fin.at[pl.ds(0, NT - 1)], f_recv)
    total = jnp.sum(fin[...], axis=0)
    per = 128 // RK
    row = lax.broadcasted_iota(I32, (8, 128), 0)
    turn = lax.rem(128 - lax.rem(tile, per) * RK, 128)
    for out, base, add in ((out_mid, 0, None), (out_low, 4, lbuf)):
        line = jnp.sum(jnp.where(row == base + tile // per, total, 0.0), axis=0, keepdims=True)
        line = pltpu.roll(jnp.broadcast_to(line, (8, 128)), turn, 1)[0:1, :RK]
        out[...] = line if add is None else line + add[...]

    wait(fin.at[pl.ds(0, NT - 1)], f_send)
    wait(pmbuf.at[pl.ds(0, 3)], p_send)
    wait(ygath.at[pl.ds(0, NY - 1)], y_send)
    wait(stage, x_send)
    for w in whole:
        wait(w.at[pl.ds(0, NZ - 1)], z_send)
        wait(w.at[pl.ds(0, NZ)], c_send)


def body(parent_cov, parent_map, front_rows, rows_mid, rows_low, factor_mid, dinv_mid, factor_low, diag_low):
    vm, sm, hb = (pl.BlockSpec(memory_space=s) for s in (pltpu.VMEM, pltpu.SMEM, pl.ANY))
    dma = pltpu.SemaphoreType.DMA
    return pl.pallas_call(
        kernel,
        out_shape=[jax.ShapeDtypeStruct((1, RK), F32)] * 2,
        in_specs=[sm, sm] + [hb] * 7,
        out_specs=[vm, vm],
        scratch_shapes=[
            pltpu.VMEM((NY, NP, CB, RB), F32),
            pltpu.VMEM((NX - 1, NY, CB, RB), F32),
            pltpu.VMEM((NL, CB, RB), F32),
            pltpu.VMEM((NX, 8, 128), I32),
            pltpu.VMEM((NT, RF, S), F32),
            pltpu.VMEM((NT, RF, S), F32),
            pltpu.VMEM((2, M), I32),
            pltpu.VMEM((RK, S), F32),
            pltpu.VMEM((1, RK), F32),
            pltpu.VMEM((NB, WIN, BLK), BF),
            pltpu.VMEM((NZ, WIN, PL), BF),
            pltpu.VMEM((2 * RB, F), BF),
            pltpu.VMEM((ROWS, F), BF),
            pltpu.VMEM((NZ, ROWS, PL), BF),
            pltpu.VMEM((M, S), BF),
            pltpu.VMEM((M, S), BF),
            pltpu.VMEM((ROWS, S), F32),
            pltpu.VMEM((TOPL, S), F32),
            pltpu.VMEM((NT, 8, 128), F32),
            dma, dma((2, 14)), dma, dma, dma, dma, dma, dma((2, NPIECE)), dma, dma((2, 5)), dma, dma, dma((7,)),
        ],
        compiler_params=pltpu.CompilerParams(
            collective_id=0, has_side_effects=True, vmem_limit_bytes=60 * 1024 * 1024
        ),
        cost_estimate=pl.CostEstimate(flops=5 * 10**9, bytes_accessed=10**6, transcendentals=0),
    )(
        parent_map, front_rows, jnp.swapaxes(parent_cov, 1, 2), rows_mid, rows_low,
        factor_mid[0], dinv_mid[0], factor_low[0], diag_low,
    )


def solution(mesh):
    return jax.shard_map(
        body,
        mesh=mesh,
        in_specs=(
            P(None, "tile", "leaf"),
            P("leaf"),
            P("leaf", None),
            P("leaf", None),
            P("leaf", None),
            P("leaf", "tile", None),
            P("leaf", "tile", None),
            P("leaf", "tile", None),
            P("leaf", "tile"),
        ),
        out_specs=(P("leaf", "tile"), P("leaf", "tile")),
        check_vma=False,
    )
```

time: 62.4 us -> 59.4 us (0.952)
  local copies, waits for them, and re-layouts: 4.34 us -> 1.8 us
    unnamed x17 -> x6, local copies, waits for them, and re-layouts: 4.34 us -> 1.8 us
where the time goes in v2:
time: 59.4 us; the launch traced here: 59.3 us
  Pallas kernels  56.2 us (95%)
  local copies, waits for them, and re-layouts  1.8 us (3%)
  between operations  1.3 us (2%)
    pallas_call x1, Pallas kernels, body(): pl.pallas_call(kernel, out_shape=[jax.ShapeDtypeStruct((1, RK), F32)] * 2...  56.2 us
    unnamed x6, local copies, waits for them, and re-layouts  1.8 us

profile of v2, /device:TPU:1, one launch (start us, length us, event | category | flops | bytes accessed | tf_op | source)
XLA Modules:
  0.0 59.3 jit_solution(12758634166966659207)
XLA Ops:
  1.3 56.2 %shard_map.104 = (f32[1,32]{1,0:T(1,128)}, f32[1,32]{1,0:T(1,128)}) custom-call(s32[1]{0:T(128)S(6)} %copy.13.pmap, s32[1,2]{1,0:T(1,128)} %counts.1, f32[4,64,128]{2,1,0:T(8,128)} %bitcast.6, s32[1,1536]{1,0:T(1,128)} %rows_mid.1, s32[1,1536]{1,0:T(1,128)} %rows_low.1, f32[96,512]{1,0:T(8,128)} %bitcast.4, f32[32,512]{1,0:T(8,128)} %bitcast.7, ...), custom_call_target="tpu_custom_call" | custom-call | flops 5000000000 | bytes 1000000 | tf_op jit(solution)/shard_map/pallas_call | solution.py:320
  57.4 0.0 copy-start.1
  57.5 0.7 %copy-done.1 = f32[1,32]{1,0:T(1,128)S(1)} copy-done((f32[1,32]{1,0:T(1,128)S(1)}, f32[1,32]{1,0:T(1,128)}, u32[]{:S(2)}) %copy-start.1) | copy-done | bytes 152
  58.1 0.0 copy-start
  58.1 0.5 copy.14
  58.6 0.1 copy-done
  58.7 0.5 copy.15
Async XLA Ops:
  57.4 0.7 %copy-start.1 = (f32[1,32]{1,0:T(1,128)S(1)}, f32[1,32]{1,0:T(1,128)}, u32[]{:S(2)}) copy-start(f32[1,32]{1,0:T(1,128)} %get-tuple-element.4) | copy-start | bytes 388
  58.1 0.6 %copy-start = (f32[1,32]{1,0:T(1,128)S(1)}, f32[1,32]{1,0:T(1,128)}, u32[]{:S(2)}) copy-start(f32[1,32]{1,0:T(1,128)} %get-tuple-element.5) | copy-start | bytes 388

commit v3 on v2

--- a/solution.py
+++ b/solution.py
@@ -17,7 +17,7 @@
 NB = M // BLK
 BF, F32, I32 = jnp.bfloat16, jnp.float32, jnp.int32
 MESH = pl.DeviceIdType.MESH
-AHEAD = 9
+AHEAD, LAG = 4, 1
 
 TOP, BOT, DI, ID, TOPL, BOTL, DIL, ROWS = 0, RB, 2 * RB, 2 * RB + RK, 2 * RB + 2 * RK, 3 * RB + 2 * RK, 4 * RB + 2 * RK, 4 * RB + 3 * RK
 
@@ -25,12 +25,12 @@
 def ring_order():
     def pieces(a, s):
         if s < 3:
-            return [(a, s, 0, 32), (a, s, 32, 32), (a, s, 64, 32)]
-        return [(a, s, 0, 32), (a, s, 32, 16)]
+            return [(a, s, 0, 48), (a, s, 48, 48)]
+        return [(a, s, 0, 48)]
 
     up = []
-    for s in range(5):
-        up += (pieces(0, s) if s < 4 else []) + (pieces(1, s - 1) if s > 0 else [])
+    for s in range(4 + LAG):
+        up += (pieces(0, s) if s < 4 else []) + (pieces(1, s - LAG) if s >= LAG else [])
     down = [(a, s, RF - r - n, n) for a, s, r, n in up]
     return up, down
 
@@ -54,9 +54,9 @@
 
 
 def kernel(
-    pmap, counts, cov, rows_mid, rows_low, fm, dinv, fl, dlow,
-    out_mid, out_low,
-    ygath, stage, covsel, pmbuf, xm, xl, rbuf, dbuf, lbuf, qoh, roh, csrc, u, v, fhi, flo, yhi, ylo, fin,
+    pmap_hbm, counts_hbm, cov, rows_mid, rows_low, fm, dinv, fl, dlow,
+    out,
+    ygath, stage, covsel, pmbuf, xm, xl, rbuf, dbuf, lbuf, qoh, roh, csrc, u, v, fhi, flo, yhi, ylo, fin, pmap, counts,
     y_send, y_recv, x_send, x_recv, p_send, p_recv, z_send, z_recv, c_send, c_recv, f_send, f_recv, l_sem,
 ):
     leaf, tile = lax.axis_index("leaf"), lax.axis_index("tile")
@@ -80,14 +80,15 @@
     for other in near:
         pl.semaphore_signal(barrier, inc=1, device_id=other, device_id_type=MESH)
 
+    parent = pltpu.make_async_copy(pmap_hbm, pmap, l_sem.at[8])
+    parent.start()
     local = [
         (cov, ygath.at[y]), (rows_mid, rbuf.at[0:1]), (rows_low, rbuf.at[1:2]), (dinv, dbuf), (dlow, lbuf),
-        (fm, xm.at[tile]), (fl, xl.at[tile]),
+        (counts_hbm, counts), (fm, xm.at[tile]), (fl, xl.at[tile]),
     ]
     local = [pltpu.make_async_copy(src, dst, l_sem.at[i]) for i, (src, dst) in enumerate(local)]
     for copy in local:
         copy.start()
-    pmbuf[x] = jnp.full((8, 128), pmap[0], I32)
     pl.semaphore_wait(barrier, len(near))
 
     def send(src, dst, ssem, rsem, where):
@@ -99,8 +100,8 @@
         pltpu.make_async_copy(ref, ref, sem).wait()
 
     def y_piece(d, j):
-        s, p = divmod(j, NP)
-        return s, (p if d == 0 else NP - 1 - p)
+        s, p = divmod(j, 2)
+        return s, pl.ds(2 * (p if d == 0 else 1 - p), 2)
 
     def y_go(d, j):
         s, p = y_piece(d, j)
@@ -121,19 +122,21 @@
         a, s, r, n = (UP, DOWN)[d][k]
         wait(whole[a].at[zt(-s - 1 if d == 0 else s + 1), pl.ds(r, n)], z_recv.at[d, k])
 
+    parent.wait()
+    pmbuf[x] = jnp.full((8, 128), pmap[0], I32)
     for dx in (1, 2, 3):
         send(pmbuf.at[x], pmbuf.at[x], p_send, p_recv, (leaf_at(dx, 0), tile))
-    for j in range(NP):
-        y_go(0, j)
-        y_go(1, j)
-    due = {}
+    due = ({}, {})
     for d, seq in ((0, UP), (1, DOWN)):
         for k in range(NPIECE):
             after = k - AHEAD if seq[k][1] == 0 else max(k - AHEAD, source_of(seq, k))
             if after < 0:
                 z_go(d, k)
             else:
-                due.setdefault(after, []).append((d, k))
+                due[d].setdefault(after, []).append(k)
+    for j in range(2):
+        y_go(0, j)
+        y_go(1, j)
     for a in range(2):
         send(own[a], whole[a].at[tile], c_send, c_recv.at[a, 0], (leaf, sibling))
 
@@ -180,7 +183,7 @@
                 send(stage.at[dx - 1, ys], covsel.at[x * NY + ys], x_send, x_recv, (leaf_at(dx, 0), tile))
 
     def pass_on(a, s):
-        for t in (zt(-s), zt(s))[: 2 if s < 4 else 1]:
+        for t in (zt(-s), zt(s)):
             send(whole[a].at[t], whole[a].at[t], c_send, c_recv.at[a, s], (leaf, sibling))
 
     def parent_columns():
@@ -235,54 +238,58 @@
     wait(pmbuf.at[pl.ds(0, 3)], p_recv)
     choose(y)
 
-    beside = {}
+    todo = [[] for _ in range(NPIECE)]
 
     def at(k, f, *args):
-        beside.setdefault(k, []).append((f, args))
+        todo[k].append((f, args))
 
     for b in range(NB):
-        at(3 + b, mid_onehot, b)
+        at(b // 3, mid_onehot, b)
     for p in range(NZ):
-        at(4 + p, low_onehot, p)
-    at(8, mid_halves, 0)
-    at(9, mid_halves, 1)
-    at(10, mid_halves, 2)
-    at(12, parent_columns)
+        at(2 + p // 4, low_onehot, p)
+    at(4, mid_halves, 0)
+    at(5, mid_halves, 1)
+    at(7, mid_halves, 2)
+    at(8, parent_columns)
     for p in range(3, NZ):
-        at(13, pick, p)
-    at(14, mid_halves, 3)
-    at(17, mid_halves, 4)
-    at(17, cross_rows)
+        at(9, pick, p)
+    at(9, mid_halves, 3)
+    at(10, mid_halves, 4)
+    at(10, cross_rows)
     for p in range(3):
-        at(17, pick, p)
-    for s in range(3):
-        at(18, low_terms, s)
-    at(19, low_terms, 3)
-    at(21, low_terms, 4)
-
-    ny = 3 * NP + NP // 2
+        at(11, pick, p)
+    at(11, low_terms, 0)
+    at(12, low_terms, 1)
+    at(12, low_terms, 2)
+    at(13, low_terms, 3)
+    at(13, low_terms, 4)
+
+    ny = 7
     jy = 0
     for k in range(NPIECE):
-        while jy < ny and jy <= 2 * k:
+        while jy < ny and jy <= k:
             for d in (0, 1):
                 y_come(d, jy)
-                if jy + NP < ny:
-                    y_go(d, jy + NP)
-            s, p = divmod(jy, NP)
-            if s < 3 and p == NP - 1:
+                if jy + 2 < ny:
+                    y_go(d, jy + 2)
+            s, p = divmod(jy, 2)
+            if s < 3 and p == 1:
                 choose(lax.rem(y + NY - 1 - s, NY))
                 choose(lax.rem(y + s + 1, NY))
             elif jy == ny - 1:
                 choose(lax.rem(y + NY // 2, NY))
             jy += 1
-        z_come(0, k)
-        z_come(1, k)
-        for d, q in due.get(k, ()):
-            z_go(d, q)
         a, s = UP[k][:2]
-        if k + 1 == NPIECE or UP[k + 1][:2] != (a, s):
+        for d in (0, 1):
+            z_come(d, k)
+            for q in due[d].get(k, ()):
+                z_go(d, q)
+            if s == 3:
+                half = whole[a].at[zt(4), pl.ds((UP, DOWN)[d][k][2], RF // 2)]
+                send(half, half, c_send, c_recv.at[a, 4], (leaf, sibling))
+        if s < 3 and UP[k + 1][:2] != (a, s):
             pass_on(a, s + 1)
-        for f, args in beside.get(k, ()):
+        for f, args in todo[k]:
             f(*args)
 
     def rows(r0, rl, n):
@@ -300,10 +307,10 @@
     per = 128 // RK
     row = lax.broadcasted_iota(I32, (8, 128), 0)
     turn = lax.rem(128 - lax.rem(tile, per) * RK, 128)
-    for out, base, add in ((out_mid, 0, None), (out_low, 4, lbuf)):
+    for o, base, add in ((0, 0, None), (1, 4, lbuf)):
         line = jnp.sum(jnp.where(row == base + tile // per, total, 0.0), axis=0, keepdims=True)
         line = pltpu.roll(jnp.broadcast_to(line, (8, 128)), turn, 1)[0:1, :RK]
-        out[...] = line if add is None else line + add[...]
+        out[o : o + 1] = line if add is None else line + add[...]
 
     wait(fin.at[pl.ds(0, NT - 1)], f_send)
     wait(pmbuf.at[pl.ds(0, 3)], p_send)
@@ -315,13 +322,13 @@
 
 
 def body(parent_cov, parent_map, front_rows, rows_mid, rows_low, factor_mid, dinv_mid, factor_low, diag_low):
-    vm, sm, hb = (pl.BlockSpec(memory_space=s) for s in (pltpu.VMEM, pltpu.SMEM, pl.ANY))
+    vm, hb = (pl.BlockSpec(memory_space=s) for s in (pltpu.VMEM, pl.ANY))
     dma = pltpu.SemaphoreType.DMA
-    return pl.pallas_call(
+    out = pl.pallas_call(
         kernel,
-        out_shape=[jax.ShapeDtypeStruct((1, RK), F32)] * 2,
-        in_specs=[sm, sm] + [hb] * 7,
-        out_specs=[vm, vm],
+        out_shape=jax.ShapeDtypeStruct((2, RK), F32),
+        in_specs=[hb] * 9,
+        out_specs=vm,
         scratch_shapes=[
             pltpu.VMEM((NY, NP, CB, RB), F32),
             pltpu.VMEM((NX - 1, NY, CB, RB), F32),
@@ -342,7 +349,9 @@
             pltpu.VMEM((ROWS, S), F32),
             pltpu.VMEM((TOPL, S), F32),
             pltpu.VMEM((NT, 8, 128), F32),
-            dma, dma((2, 14)), dma, dma, dma, dma, dma, dma((2, NPIECE)), dma, dma((2, 5)), dma, dma, dma((7,)),
+            pltpu.SMEM((1,), I32),
+            pltpu.SMEM((1, 2), I32),
+            dma, dma((2, 14)), dma, dma, dma, dma, dma, dma((2, NPIECE)), dma, dma((2, 5)), dma, dma, dma((9,)),
         ],
         compiler_params=pltpu.CompilerParams(
             collective_id=0, has_side_effects=True, vmem_limit_bytes=60 * 1024 * 1024
@@ -352,6 +361,7 @@
         parent_map, front_rows, jnp.swapaxes(parent_cov, 1, 2), rows_mid, rows_low,
         factor_mid[0], dinv_mid[0], factor_low[0], diag_low,
     )
+    return out[0:1], out[1:2]
 
 
 def solution(mesh):

time: 59.4 us -> 56.7 us (0.955)
  Pallas kernels: 56.2 us -> 54.1 us
    pallas_call x1, Pallas kernels: 56.2 us -> 54.1 us  [body(): pl.pallas_call(kernel, out_shape=jax.ShapeDtypeStruct((2, RK), F32), in_s...]
    unnamed x6 -> x0, local copies, waits for them, and re-layouts: 1.8 us -> none
    slice x0 -> x1, local copies, waits for them, and re-layouts: none -> 1.25 us  [body(): return (out[0:1], out[1:2])]
where the time goes in v3:
time: 56.7 us; the launch traced here: 56.6 us
  Pallas kernels  54.1 us (95%)
  between operations  1.29 us (2%)
  local copies, waits for them, and re-layouts  1.25 us (2%)
    pallas_call x1, Pallas kernels, body(): pl.pallas_call(kernel, out_shape=jax.ShapeDtypeStruct((2, RK), F32), in_s...  54.1 us
    slice x1, local copies, waits for them, and re-layouts, body(): return (out[0:1], out[1:2])  1.25 us

profile of v3, /device:TPU:1, one launch (start us, length us, event | category | flops | bytes accessed | tf_op | source)
XLA Modules:
  0.0 56.6 jit_solution(12420908350771569351)
XLA Ops:
  1.3 54.1 %shard_map.104 = f32[2,32]{1,0:T(2,128)} custom-call(s32[1]{0:T(128)S(6)} %copy.11.pmap_hbm, s32[1,2]{1,0:T(1,128)} %counts_hbm.1, f32[4,64,128]{2,1,0:T(8,128)} %bitcast.6, s32[1,1536]{1,0:T(1,128)} %rows_mid.1, s32[1,1536]{1,0:T(1,128)} %rows_low.1, f32[96,512]{1,0:T(8,128)} %bitcast.4, f32[32,512]{1,0:T(8,128)} %bitcast.7, f32[96,512]{1,0:T(8,128)} %bitcast.5, ...), custom_call_target="tpu_custom_call" | custom-call | flops 5000000000 | bytes 1000000 | tf_op jit(solution)/shard_map/pallas_call | solution.py:327
  55.3 1.3 %fusion = (f32[1,32]{1,0:T(1,128)}, f32[1,32]{1,0:T(1,128)}) fusion(f32[2,32]{1,0:T(2,128)} %shard_map.104), kind=kLoop, calls=%fused_computation | loop fusion | bytes 512 | tf_op jit(solution)/shard_map/slice | solution.py:364

commit v4 on v3

--- a/solution.py
+++ b/solution.py
@@ -87,8 +87,6 @@
         (counts_hbm, counts), (fm, xm.at[tile]), (fl, xl.at[tile]),
     ]
     local = [pltpu.make_async_copy(src, dst, l_sem.at[i]) for i, (src, dst) in enumerate(local)]
-    for copy in local:
-        copy.start()
     pl.semaphore_wait(barrier, len(near))
 
     def send(src, dst, ssem, rsem, where):
@@ -122,13 +120,9 @@
         a, s, r, n = (UP, DOWN)[d][k]
         wait(whole[a].at[zt(-s - 1 if d == 0 else s + 1), pl.ds(r, n)], z_recv.at[d, k])
 
-    parent.wait()
-    pmbuf[x] = jnp.full((8, 128), pmap[0], I32)
-    for dx in (1, 2, 3):
-        send(pmbuf.at[x], pmbuf.at[x], p_send, p_recv, (leaf_at(dx, 0), tile))
     due = ({}, {})
-    for d, seq in ((0, UP), (1, DOWN)):
-        for k in range(NPIECE):
+    for k in range(NPIECE):
+        for d, seq in ((0, UP), (1, DOWN)):
             after = k - AHEAD if seq[k][1] == 0 else max(k - AHEAD, source_of(seq, k))
             if after < 0:
                 z_go(d, k)
@@ -137,6 +131,12 @@
     for j in range(2):
         y_go(0, j)
         y_go(1, j)
+    parent.wait()
+    pmbuf[x] = jnp.full((8, 128), pmap[0], I32)
+    for dx in (1, 2, 3):
+        send(pmbuf.at[x], pmbuf.at[x], p_send, p_recv, (leaf_at(dx, 0), tile))
+    for copy in local:
+        copy.start()
     for a in range(2):
         send(own[a], whole[a].at[tile], c_send, c_recv.at[a, 0], (leaf, sibling))
 
@@ -250,9 +250,9 @@
     at(4, mid_halves, 0)
     at(5, mid_halves, 1)
     at(7, mid_halves, 2)
-    at(8, parent_columns)
+    at(7, parent_columns)
     for p in range(3, NZ):
-        at(9, pick, p)
+        at(8, pick, p)
     at(9, mid_halves, 3)
     at(10, mid_halves, 4)
     at(10, cross_rows)

time: 56.7 us -> 56.6 us (level)
  no operation moved by 1% of the time
where the time goes in v4:
time: 56.6 us; the launch traced here: 56.4 us
  Pallas kernels  53.9 us (95%)
  between operations  1.29 us (2%)
  local copies, waits for them, and re-layouts  1.25 us (2%)
    pallas_call x1, Pallas kernels, body(): pl.pallas_call(kernel, out_shape=jax.ShapeDtypeStruct((2, RK), F32), in_s...  53.9 us
    slice x1, local copies, waits for them, and re-layouts, body(): return (out[0:1], out[1:2])  1.25 us

profile of v4, /device:TPU:1, one launch (start us, length us, event | category | flops | bytes accessed | tf_op | source)
XLA Modules:
  0.0 56.4 jit_solution(6130611135862640032)
XLA Ops:
  1.3 53.9 %shard_map.104 = f32[2,32]{1,0:T(2,128)} custom-call(s32[1]{0:T(128)S(6)} %copy.11.pmap_hbm, s32[1,2]{1,0:T(1,128)} %counts_hbm.1, f32[4,64,128]{2,1,0:T(8,128)} %bitcast.6, s32[1,1536]{1,0:T(1,128)} %rows_mid.1, s32[1,1536]{1,0:T(1,128)} %rows_low.1, f32[96,512]{1,0:T(8,128)} %bitcast.4, f32[32,512]{1,0:T(8,128)} %bitcast.7, f32[96,512]{1,0:T(8,128)} %bitcast.5, ...), custom_call_target="tpu_custom_call" | custom-call | flops 5000000000 | bytes 1000000 | tf_op jit(solution)/shard_map/pallas_call | solution.py:327
  55.2 1.3 %fusion = (f32[1,32]{1,0:T(1,128)}, f32[1,32]{1,0:T(1,128)}) fusion(f32[2,32]{1,0:T(2,128)} %shard_map.104), kind=kLoop, calls=%fused_computation | loop fusion | bytes 512 | tf_op jit(solution)/shard_map/slice | solution.py:364

commit v5 on v4

--- a/solution.py
+++ b/solution.py
@@ -56,7 +56,7 @@
 def kernel(
     pmap_hbm, counts_hbm, cov, rows_mid, rows_low, fm, dinv, fl, dlow,
     out,
-    ygath, stage, covsel, pmbuf, xm, xl, rbuf, dbuf, lbuf, qoh, roh, csrc, u, v, fhi, flo, yhi, ylo, fin, pmap, counts,
+    ygath, stage, covsel, pmbuf, xm, xl, rbuf, dbuf, lbuf, qoh, roh, csrc, u, v, fhi, flo, yhi, fin, pmap, counts,
     y_send, y_recv, x_send, x_recv, p_send, p_recv, z_send, z_recv, c_send, c_recv, f_send, f_recv, l_sem,
 ):
     leaf, tile = lax.axis_index("leaf"), lax.axis_index("tile")
@@ -219,8 +219,9 @@
             hi, lo = split(xl[pl.ds(p * NC, NC)].reshape(PL, S))
             left = v[p]
             first, second = dot(left, hi), dot(left[:TOPL], lo)
-            yhi[...] = first if s == 0 else yhi[...] + first
-            ylo[...] = second if s == 0 else ylo[...] + second
+            for r0, add in ((0, first[:TOPL] + second), (TOPL, first[TOPL:])):
+                part = slice(r0, r0 + add.shape[0])
+                yhi[part] = add if s == 0 else yhi[part] + add
 
     def cross_rows():
         both = dot(u[: 2 * RB, S:], fhi[...]) + dot(u[: 2 * RB, S:], flo[...])
@@ -244,9 +245,9 @@
         todo[k].append((f, args))
 
     for b in range(NB):
-        at(b // 3, mid_onehot, b)
+        at(b // 2, mid_onehot, b)
     for p in range(NZ):
-        at(2 + p // 4, low_onehot, p)
+        at(2 + p // 2, low_onehot, p)
     at(4, mid_halves, 0)
     at(5, mid_halves, 1)
     at(7, mid_halves, 2)
@@ -293,10 +294,10 @@
             f(*args)
 
     def rows(r0, rl, n):
-        return yhi[r0 : r0 + n] + yhi[rl : rl + n] + ylo[r0 : r0 + n]
+        return yhi[r0 : r0 + n] + yhi[rl : rl + n]
 
     part = jnp.sum(rows(TOP, TOPL, RB) * rows(BOT, BOTL, RB), axis=0, keepdims=True)
-    part += jnp.sum(rows(DI, DIL, RK) * (yhi[ID : ID + RK] + ylo[ID : ID + RK]), axis=0, keepdims=True)
+    part += jnp.sum(rows(DI, DIL, RK) * yhi[ID : ID + RK], axis=0, keepdims=True)
     for k in range(4):
         fin[tile, k + 4 : k + 5] = part[:, k * 128 : (k + 1) * 128]
 
@@ -347,7 +348,6 @@
             pltpu.VMEM((M, S), BF),
             pltpu.VMEM((M, S), BF),
             pltpu.VMEM((ROWS, S), F32),
-            pltpu.VMEM((TOPL, S), F32),
             pltpu.VMEM((NT, 8, 128), F32),
             pltpu.SMEM((1,), I32),
             pltpu.SMEM((1, 2), I32),

time: 56.6 us -> 56.7 us (level)
  no operation moved by 1% of the time
where the time goes in v5:
time: 56.7 us; the launch traced here: 56.5 us
  Pallas kernels  54 us (95%)
  between operations  1.29 us (2%)
  local copies, waits for them, and re-layouts  1.25 us (2%)
    pallas_call x1, Pallas kernels, body(): pl.pallas_call(kernel, out_shape=jax.ShapeDtypeStruct((2, RK), F32), in_s...  54 us
    slice x1, local copies, waits for them, and re-layouts, body(): return (out[0:1], out[1:2])  1.25 us

profile of v5, /device:TPU:1, one launch (start us, length us, event | category | flops | bytes accessed | tf_op | source)
XLA Modules:
  0.0 56.5 jit_solution(13279051195053086586)
XLA Ops:
  1.3 54.0 %shard_map.104 = f32[2,32]{1,0:T(2,128)} custom-call(s32[1]{0:T(128)S(6)} %copy.11.pmap_hbm, s32[1,2]{1,0:T(1,128)} %counts_hbm.1, f32[4,64,128]{2,1,0:T(8,128)} %bitcast.6, s32[1,1536]{1,0:T(1,128)} %rows_mid.1, s32[1,1536]{1,0:T(1,128)} %rows_low.1, f32[96,512]{1,0:T(8,128)} %bitcast.4, f32[32,512]{1,0:T(8,128)} %bitcast.7, f32[96,512]{1,0:T(8,128)} %bitcast.5, ...), custom_call_target="tpu_custom_call" | custom-call | flops 5000000000 | bytes 1000000 | tf_op jit(solution)/shard_map/pallas_call | solution.py:328
  55.3 1.3 %fusion = (f32[1,32]{1,0:T(1,128)}, f32[1,32]{1,0:T(1,128)}) fusion(f32[2,32]{1,0:T(2,128)} %shard_map.104), kind=kLoop, calls=%fused_computation | loop fusion | bytes 512 | tf_op jit(solution)/shard_map/slice | solution.py:364
